TPU v7x, 512 devices: a whole 4x4x16 slice. The times are simulated.
512 devices in a mesh: attn: 32 (over z, core), frow: 4 (over y), fcol: 4 (over x).
Axes of the slice: x: 4, y: 4, z: 16, core: 2. Of those that a mesh axis runs over, the one named last changes fastest.
Arguments:
- query_rows: bfloat16 [384, 8192], P(('attn', 'fcol'), 'frow'), may hold values from -10 to 10
- kv_cache: bfloat16 [2, 384, 1024, 512], P(None, ('attn', 'fcol'), None, 'frow'), may hold values from -16 to 16
- lengths: int32 [384], P(('attn', 'fcol')), may hold values from 1 to 1024, as said below
- residual: bfloat16 [384, 8192], P(('attn', 'fcol'), 'frow'), may hold values from -40 to 40
- norm_gain: float32 [8192], P('frow'), may hold values from 0.1 to 1.9
- w_gate_up: bfloat16 [2, 32768, 8192], P(None, ('attn', 'fcol'), 'frow'), may hold values from -0.0625 to 0.0625
- w_down: bfloat16 [32768, 8192], P(('attn', 'fcol'), 'frow'), may hold values from -0.03125 to 0.03125
Outputs:
- ffn_out: bfloat16 [384, 8192], P(('attn', 'fcol'), 'frow')
Inputs may be any that keep to these rules, and one draw needn't show every extreme that they name: `lengths`: some row has all 1024 positions filled.
All inputs are finite; a program needn't handle non-finite values.
Results may differ from a plain program's by a relative error of at most 0.014.
Values may be sent and summed in bfloat16 or wider, within the bound.
A program may use at most 64 MiB of HBM per device.

v0:
```python
import math

import jax
import jax.numpy as jnp
from jax import lax
from jax.sharding import PartitionSpec as P

HD = 128
GROUP = 16


def attend(query_rows, kv_cache, lengths):
    row_count = query_rows.shape[0]
    head_count = kv_cache.shape[3] // HD
    cache_span = kv_cache.shape[2]
    queries = query_rows.reshape(row_count, head_count, GROUP, HD)
    keys_here = kv_cache[0].reshape(row_count, cache_span, head_count, HD)
    values_here = kv_cache[1].reshape(row_count, cache_span, head_count, HD)
    scores = jnp.einsum(
        "bgqd,bpgd->bgqp", queries, keys_here, preferred_element_type=jnp.float32
    ) / math.sqrt(HD)
    live_mask = (jnp.arange(cache_span, dtype=jnp.int32)[None, :] < lengths[:, None])[
        :, None, None, :
    ]
    scores = jnp.where(live_mask, scores, -1e30)
    row_top = jnp.max(scores, axis=-1, keepdims=True)
    weights = jnp.where(live_mask, jnp.exp(scores - row_top), 0.0)
    denominator = jnp.sum(weights, axis=-1)
    numerator = jnp.einsum(
        "bgqp,bpgd->bgqd",
        weights.astype(jnp.bfloat16),
        values_here,
        preferred_element_type=jnp.float32,
    )
    return (numerator / denominator[..., None]).reshape(row_count, -1)


def normalize(mixed_rows, norm_gain):
    width = mixed_rows.shape[1] * lax.axis_size("frow")
    square_sum = lax.psum(jnp.sum(mixed_rows * mixed_rows, axis=1), "frow")
    scale = lax.rsqrt(square_sum / width + 1e-05)
    return (mixed_rows * norm_gain * scale[:, None]).astype(jnp.bfloat16)


def on_device(query_rows, kv_cache, lengths, residual, norm_gain, w_gate_up, w_down):
    attended = attend(query_rows, kv_cache, lengths)
    mixed_rows = residual.astype(jnp.float32) + attended
    normed = normalize(mixed_rows, norm_gain)
    gate_up = jnp.einsum(
        "rd,kfd->krf",
        lax.all_gather(normed, ("attn", "fcol"), axis=0, tiled=True),
        w_gate_up,
        preferred_element_type=jnp.float32,
    )
    summed = lax.psum(gate_up, "frow")
    hidden = (jax.nn.silu(summed[0]) * summed[1]).astype(jnp.bfloat16)
    ffn_sum = lax.psum_scatter(
        jnp.dot(hidden, w_down, preferred_element_type=jnp.float32),
        ("attn", "fcol"),
        scatter_dimension=0,
        tiled=True,
    )
    return ffn_sum.astype(jnp.bfloat16)


def solution(mesh):
    return jax.shard_map(
        on_device,
        mesh=mesh,
        in_specs=(
            P(("attn", "fcol"), "frow"),
            P(None, ("attn", "fcol"), None, "frow"),
            P(("attn", "fcol")),
            P(("attn", "fcol"), "frow"),
            P("frow"),
            P(None, ("attn", "fcol"), "frow"),
            P(("attn", "fcol"), "frow"),
        ),
        out_specs=P(("attn", "fcol"), "frow"),
        check_vma=False,
    )
```

profile of v0, /device:TPU:1, one launch (start us, length us, event | category | flops | bytes accessed | tf_op | source)
XLA Modules:
  0.0 762.0 jit_solution(4023453178328782170)
XLA Ops:
  6.5 0.0 copy-start
  6.5 0.0 copy-start.2
  6.5 0.0 copy-start.3
  6.5 0.0 all-gather.3.cloned.1.call-start
  6.5 0.9 iota_compare_fusion
  7.4 1.6 fusion.20
  9.1 1.3 fusion.5
  10.4 0.0 copy-done.2
  10.4 0.1 multiply_reduce_fusion
  10.6 9.6 %psum.14 = f32[3]{0:T(128)S(1)} all-reduce(f32[3]{0:T(128)S(1)} %multiply_reduce_fusion), channel_id=1, replica_groups=mesh['attn'=32,'frow'=4,'fcol'=4] {'frow'}, use_global_device_ids=true, to_apply=%region_3.4 | all-reduce | flops 3 | bytes 24 | tf_op jit(solution)/shard_map/psum | solution.py:40
  20.1 0.0 copy-done.3
  20.1 0.7 fusion.16
  20.8 0.0 all-gather.3.cloned.1.call-update
  20.8 0.0 all-reduce.4.cloned.1.call-start
  20.9 144.4 %all-gather.3.cloned.1.call-done = bf16[128,3,2048]{2,1,0:T(4,128)(2,1)} async-done(((bf16[1,3,2048]{2,1,0:T(4,128)(2,1)}), bf16[128,3,2048]{2,1,0:T(4,128)(2,1)}) %all-gather.3.cloned.1.call-update) | async-done | bytes 1572880 | tf_op jit(solution)/shard_map/all_gather | solution.py:51
  165.3 5.1 reshape.65
  170.4 0.0 copy-done
  170.4 0.0 copy-start.1
  170.4 3.4 convolution_bitcast_fusion
  173.7 0.0 all-reduce.4.cloned.1.call-update
  173.8 1.3 dynamic-slice
  175.7 52.1 %all-reduce.4.cloned.1.call-done = f32[2,384,256]{2,1,0:T(8,128)} async-done(((f32[2,384,256]{2,1,0:T(8,128)}), f32[2,384,256]{2,1,0:T(8,128)}) %all-reduce.4.cloned.1.call-update) | async-done | bytes 786448 | tf_op jit(solution)/shard_map/psum | solution.py:55
  227.8 0.0 copy-done.1
  227.8 3.4 fusion.12
  231.1 522.6 %all-reduce.5 = bf16[384,2048]{1,0:T(8,128)(2,1)} all-reduce(f32[384,2048]{1,0:T(8,128)} %fusion.12), channel_id=2, replica_groups=mesh['attn'=32,'frow'=4,'fcol'=4] {'attn','fcol'}, use_global_device_ids=true, to_apply=%region_5.6.clone | all-reduce | flops 786432 | bytes 4718592
  753.7 1.5 dynamic-slice_convert_fusion
  (1 shorter events, 0.0 us)
Async XLA Ops:
  6.5 163.8 %copy-start = (bf16[2,256,2048]{2,1,0:T(8,128)(2,1)S(1)}, bf16[2,256,2048]{2,1,0:T(8,128)(2,1)}, u32[]{:S(2)}) copy-start(bf16[2,256,2048]{2,1,0:T(8,128)(2,1)} %param.12) | copy-start | bytes 6291460
  6.5 3.9 copy-start.2
  6.5 13.6 %copy-start.3 = (f32[2048]{0:T(1024)S(1)}, f32[2048]{0:T(1024)}, u32[]{:S(2)}) copy-start(f32[2048]{0:T(1024)} %param.11) | copy-start | bytes 24580
  6.5 158.7 %all-gather.3.cloned.1.call-start = ((), (), s32[]{:S(2)}) async-start(), calls=%async_computation.1 | async-start | bytes 2113536 | tf_op jit(solution)/shard_map/all_gather | solution.py:51
  20.8 206.9 %all-reduce.4.cloned.1.call-start = ((), (), s32[]{:S(2)}) async-start(), calls=%async_computation | async-start | bytes 1572864 | tf_op jit(solution)/shard_map/psum | solution.py:55
  170.4 57.4 %copy-start.1 = (bf16[256,2048]{1,0:T(8,128)(2,1)S(1)}, bf16[256,2048]{1,0:T(8,128)(2,1)}, u32[]{:S(2)}) copy-start(bf16[256,2048]{1,0:T(8,128)(2,1)} %param.13) | copy-start | bytes 3145732
Sparse Core Ops, SparseCore 0:
  21.0 144.2 all-gather.2
  173.9 53.8 all-reduce.3
where the time goes:
time: 766 us; the launch traced here: 762 us
  blocking collectives  532 us (69%)
  waiting for transfers between devices  197 us (26%)
  between operations  14.1 us (2%)
  matrix products  9.74 us (1%)
  local copies, waits for them, and re-layouts  7.81 us (1%)
    unnamed x1, blocking collectives  523 us
    all_gather x1, waiting for transfers between devices, on_device(): lax.all_gather(normed, ('attn', 'fcol'), axis=0, tiled=True)  144 us
    psum x1, waiting for transfers between devices, on_device(): summed = lax.psum(gate_up, 'frow')  52.1 us
  transfers between devices with their start and end apart: 2, of which 2 were waited for; matrix products, arithmetic and copies ran while one was open for 0% of the time, Pallas kernels for 0%

commit v1 on v0

v1 whole, which is shorter than its diff:
```python
import functools
import math

import jax
import jax.numpy as jnp
from jax import lax
from jax.experimental import pallas as pl
from jax.experimental.pallas import tpu as pltpu
from jax.sharding import PartitionSpec as P

HD = 128
GROUP = 16
MESH = pl.DeviceIdType.MESH
NT = (((1,), (1,)), ((), ()))

Z_OFFSETS = (0, 1, -1, 2, -2, 3, -3, 4, -4, 5, -5, 6, -6, 7, -7, 8)
Z_SLOT = {o % 16: i for i, o in enumerate(Z_OFFSETS)}
R_OFFSETS = (0, 1, -1, 2)
R_SLOT = {o % 4: i for i, o in enumerate(R_OFFSETS)}
NEAR_RUNS = ((0, 0, 1), (0, 1, 3), (0, 3, 5), (0, 5, 8))
FAR_RUNS = ((1, 0, 1), (1, 1, 3), (1, 3, 5), (1, 5, 8))


def body(len_ref, q_ref, res_ref, gain_ref, kv_hbm, wgu_hbm, wd_hbm, out_ref,
         kv, wgu, wd, lay, xb, xt, gu, yr, hb, po, dr, xr, s1, zi, zacc, zf,
         local_sem, send_sem, recv_sem):
    attn = lax.axis_index("attn")
    y = lax.axis_index("frow")
    x = lax.axis_index("fcol")
    z, core = attn // 2, attn % 2

    def at_z(offset):
        return {"attn": ((z + offset + 16) % 16) * 2 + core}

    def at_x(offset):
        return {"fcol": (x + offset + 4) % 4}

    def at_y(offset):
        return {"frow": (y + offset + 4) % 4}

    other_core = {"attn": z * 2 + 1 - core}

    loads = [
        pltpu.make_async_copy(kv_hbm, kv, local_sem.at[0]),
        pltpu.make_async_copy(wgu_hbm, wgu, local_sem.at[1]),
        pltpu.make_async_copy(wd_hbm, wd, local_sem.at[2]),
    ]
    for load in loads:
        load.start()

    barrier = pltpu.get_barrier_semaphore()
    peers = [at_z(o) for o in (4, -4, 3, -3, 2, -2, 1, -1)]
    peers += [at_x(o) for o in R_OFFSETS[1:]] + [at_y(o) for o in R_OFFSETS[1:]] + [other_core]
    for peer in peers:
        pl.semaphore_signal(barrier, inc=1, device_id=peer, device_id_type=MESH)

    started = []

    def send(src, dst, peer):
        index = len(started)
        copy = pltpu.make_async_remote_copy(
            src_ref=src, dst_ref=dst, send_sem=send_sem.at[index], recv_sem=recv_sem.at[index],
            device_id=peer, device_id_type=MESH,
        )
        copy.start()
        started.append(copy)
        return copy

    def spread(rows):
        for r in range(3):
            for h in range(GROUP):
                lay[pl.ds(r * GROUP + h, 1), :] = rows[r:r + 1, h * HD:(h + 1) * HD]
        return lay[...]

    queries = spread(q_ref[...].astype(jnp.float32)).astype(jnp.bfloat16)
    residual = spread(res_ref[...].astype(jnp.float32))
    gain = gain_ref[...]
    inverse = 1.0 / (gain * gain)
    rows_i = lax.broadcasted_iota(jnp.int32, (256, 256), 0)
    cols_i = lax.broadcasted_iota(jnp.int32, (256, 256), 1)
    swap = jnp.where(cols_i == (rows_i & 15) * 16 + (rows_i >> 4), 1.0, 0.0).astype(jnp.bfloat16)
    loads[0].wait()
    positions = lax.broadcasted_iota(jnp.int32, (GROUP, kv.shape[2]), 1)
    for r in range(3):
        scores = lax.dot_general(
            queries[r * GROUP:(r + 1) * GROUP], kv[0, r], NT, preferred_element_type=jnp.float32
        ) * (1.0 / math.sqrt(HD))
        live = positions < len_ref[r]
        scores = jnp.where(live, scores, -1e30)
        top = jnp.max(scores, axis=1, keepdims=True)
        expo = jnp.where(live, jnp.exp(scores - top), 0.0)
        total = jnp.sum(expo, axis=1, keepdims=True)
        summed = jnp.dot(expo.astype(jnp.bfloat16), kv[1, r], preferred_element_type=jnp.float32)
        mixed = residual[r * GROUP:(r + 1) * GROUP] + summed / total
        xb[0, 0, 0, 0, r * GROUP:(r + 1) * GROUP, :] = (mixed * gain).astype(jnp.bfloat16)

    pl.semaphore_wait(barrier, len(peers))

    def slot(offset):
        index = Z_SLOT[offset % 16]
        return xb.at[0, index // 8, 0, index % 8]

    z_copy = {}
    for o in (4, -4, 3, -3, 2, -2, 1, -1):
        z_copy[-o % 16] = send(slot(0), slot(-o), at_z(o))

    x_copy = {}

    def hand_on_x(run):
        chunk, first, end = run
        for k in range(first, end):
            offset = Z_OFFSETS[chunk * 8 + k]
            if offset not in (0, 4, -4):
                z_copy[offset % 16].wait_recv()
        n = end - first
        x_copy[run] = [
            send(xb.at[0, chunk, 0, pl.ds(first, n)], xb.at[0, chunk, R_SLOT[-o % 4], pl.ds(first, n)], at_x(o))
            for o in R_OFFSETS[1:]
        ]

    core_copy = {}

    def hand_on_core(run):
        chunk, first, end = run
        for copy in x_copy[run]:
            copy.wait_recv()
        here = (chunk, slice(None), pl.ds(first, end - first))
        core_copy[run] = send(xb.at[(0,) + here], xb.at[(1,) + here], other_core)

    hand_on_x(NEAR_RUNS[0])
    hand_on_x(NEAR_RUNS[1])
    hand_on_x(NEAR_RUNS[2])
    z_copy[-4 % 16].wait_recv()
    for j in (4, 3, 2, 1):
        z_copy[-(4 + j) % 16] = send(slot(-4), slot(-(4 + j)), at_z(j))
    z_copy[4].wait_recv()
    for j in (3, 2, 1):
        z_copy[4 + j] = send(slot(4), slot(4 + j), at_z(-j))
    hand_on_x(NEAR_RUNS[3])
    hand_on_x(FAR_RUNS[0])
    hand_on_core(NEAR_RUNS[0])
    hand_on_core(NEAR_RUNS[1])
    hand_on_x(FAR_RUNS[1])
    hand_on_core(NEAR_RUNS[2])
    hand_on_x(FAR_RUNS[2])
    hand_on_core(NEAR_RUNS[3])
    hand_on_x(FAR_RUNS[3])

    def widen(chunk, p):
        flat = xb[p, chunk].reshape(6, 256, HD)
        squares = []
        for g in range(6):
            turned = jnp.dot(swap, flat[g], preferred_element_type=jnp.float32)
            acc = jnp.zeros((16, HD), jnp.float32)
            for h in range(GROUP):
                part = turned[h * 16:(h + 1) * 16]
                acc += part * part * inverse[h:h + 1]
                xt[chunk, pl.ds((p * 6 + g) * 16, 16), h * HD:(h + 1) * HD] = part.astype(jnp.bfloat16)
            squares.append(jnp.sum(acc, axis=1, keepdims=True))
        return jnp.concatenate(squares, axis=0)

    lanes = lax.broadcasted_iota(jnp.int32, (96, HD), 1)

    def project(chunk, squares):
        for p in range(2):
            high = squares[p].astype(jnp.bfloat16).astype(jnp.float32)
            both = jnp.where(lanes < 64, high, squares[p] - high).astype(jnp.bfloat16)
            gu[chunk, 2 * p:2 * p + 2, :, 512:640] = both.reshape(2, 48, HD)
        rows = xt[chunk]
        for k in range(2):
            part = lax.dot_general(rows, wgu[k], NT, preferred_element_type=jnp.float32)
            gu[chunk, :, :, k * 256:(k + 1) * 256] = part.astype(jnp.bfloat16).reshape(4, 48, 256)
        return [
            send(gu.at[chunk, (y + o + 4) % 4], yr.at[chunk, R_SLOT[-o % 4] - 1], at_y(o))
            for o in R_OFFSETS[1:]
        ]

    def activate(chunk, copies):
        for copy in copies:
            copy.wait_recv()
        v = gu[chunk, y].astype(jnp.float32)
        for i in range(3):
            v += yr[chunk, i].astype(jnp.float32)
        meansq = (v[:, 512:513] + v[:, 576:577]) * (1.0 / 8192)
        scale = lax.rsqrt(meansq + 1e-05)
        gate = v[:, :256] * scale
        up = v[:, 256:512] * scale
        hb[chunk, y] = (gate / (1.0 + jnp.exp(-gate)) * up).astype(jnp.bfloat16)
        return [send(hb.at[chunk, y], hb.at[chunk, y], at_y(o)) for o in R_OFFSETS[1:]]

    def down(chunk, copies):
        for copy in copies:
            copy.wait_recv()
        for p in (1, 0):
            rows = hb[chunk, 2 * p:2 * p + 2].reshape(96, 256)
            wide = jnp.dot(rows, wd[...], preferred_element_type=jnp.float32).astype(jnp.bfloat16)
            for g in range(6):
                tall = jnp.concatenate(
                    [wide[g * 16:(g + 1) * 16, h * HD:(h + 1) * HD] for h in range(GROUP)], axis=0
                )
                turned = jnp.dot(swap, tall, preferred_element_type=jnp.float32).astype(jnp.bfloat16)
                po[p, chunk, pl.ds(g * 256, 256), :] = turned
            if p == 1:
                copy = send(po.at[1, chunk], dr.at[chunk], other_core)
        return copy

    def reduce_core(chunk, copy):
        copy.wait_recv()
        po[0, chunk] = (po[0, chunk].astype(jnp.float32) + dr[chunk].astype(jnp.float32)).astype(jnp.bfloat16)
        return [
            send(po.at[0, chunk, pl.ds(R_SLOT[o % 4] * 384, 384)], xr.at[chunk, R_SLOT[-o % 4] - 1], at_x(o))
            for o in R_OFFSETS[1:]
        ]

    def reduce_x(chunk, copies):
        for copy in copies:
            copy.wait_recv()
        v = po[0, chunk, 0:384].astype(jnp.float32)
        for i in range(3):
            v += xr[chunk, i].astype(jnp.float32)
        s1[chunk] = v.astype(jnp.bfloat16).reshape(8, 48, HD)

    loads[1].wait()
    squares_0 = [widen(0, 0)]
    for run in FAR_RUNS[:3]:
        hand_on_core(run)
    for run in NEAR_RUNS:
        core_copy[run].wait_recv()
    squares_0.append(widen(0, 1))
    hand_on_core(FAR_RUNS[3])
    y_0 = project(0, squares_0)
    squares_1 = [widen(1, 0)]
    for run in FAR_RUNS:
        core_copy[run].wait_recv()
    squares_1.append(widen(1, 1))
    y_1 = project(1, squares_1)
    h_0 = activate(0, y_0)
    h_1 = activate(1, y_1)
    loads[2].wait()
    c_0 = down(0, h_0)
    c_1 = down(1, h_1)
    x_0 = reduce_core(0, c_0)
    x_1 = reduce_core(1, c_1)

    def sums(offset):
        index = Z_SLOT[offset % 16]
        return s1.at[index // 8, index % 8]

    last = []
    reduce_x(0, x_0)
    for i, o in enumerate((3, -3, 2, -2, 1, -1)):
        last.append(send(sums(o), zf.at[i], at_z(o)))
    reduce_x(1, x_1)
    ahead = [send(sums(4 + j), zi.at[j - 1], at_z(j)) for j in (4, 3, 2, 1)]
    behind = [send(sums(-4 - j), zi.at[3 + j], at_z(-j)) for j in (3, 2, 1)]
    for copies, offset, first, count, i in ((ahead, 4, 0, 4, 6), (behind, -4, 4, 3, 7)):
        for copy in copies:
            copy.wait_recv()
        v = sums(offset)[...].astype(jnp.float32)
        for j in range(count):
            v += zi[first + j].astype(jnp.float32)
        zacc[i - 6] = v.astype(jnp.bfloat16)
        last.append(send(zacc.at[i - 6], zf.at[i], at_z(offset)))
    v = sums(0)[...].astype(jnp.float32)
    for i, copy in enumerate(last):
        copy.wait_recv()
        v += zf[i].astype(jnp.float32)
    lay[...] = v
    for r in range(3):
        for h in range(GROUP):
            out_ref[r:r + 1, h * HD:(h + 1) * HD] = lay[pl.ds(r * GROUP + h, 1), :].astype(jnp.bfloat16)
    for copy in started:
        copy.wait_send()


def on_device(query_rows, kv_cache, lengths, residual, norm_gain, w_gate_up, w_down):
    bf16 = jnp.bfloat16
    vmem = pl.BlockSpec(memory_space=pltpu.VMEM)
    hbm = pl.BlockSpec(memory_space=pl.ANY)
    return pl.pallas_call(
        body,
        out_shape=jax.ShapeDtypeStruct(query_rows.shape, bf16),
        in_specs=[pl.BlockSpec(memory_space=pltpu.SMEM), vmem, vmem, vmem, hbm, hbm, hbm],
        out_specs=vmem,
        scratch_shapes=[
            pltpu.VMEM(kv_cache.shape, bf16),
            pltpu.VMEM(w_gate_up.shape, bf16),
            pltpu.VMEM(w_down.shape, bf16),
            pltpu.VMEM((48, HD), jnp.float32),
            pltpu.VMEM((2, 2, 4, 8, 48, HD), bf16),
            pltpu.VMEM((2, 192, 2048), bf16),
            pltpu.VMEM((2, 4, 48, 640), bf16),
            pltpu.VMEM((2, 3, 48, 640), bf16),
            pltpu.VMEM((2, 4, 48, 256), bf16),
            pltpu.VMEM((2, 2, 1536, HD), bf16),
            pltpu.VMEM((2, 1536, HD), bf16),
            pltpu.VMEM((2, 3, 384, HD), bf16),
            pltpu.VMEM((2, 8, 48, HD), bf16),
            pltpu.VMEM((7, 48, HD), bf16),
            pltpu.VMEM((2, 48, HD), bf16),
            pltpu.VMEM((8, 48, HD), bf16),
            pltpu.SemaphoreType.DMA((3,)),
            pltpu.SemaphoreType.DMA((96,)),
            pltpu.SemaphoreType.DMA((96,)),
        ],
        compiler_params=pltpu.CompilerParams(
            collective_id=0, has_side_effects=True, vmem_limit_bytes=40 * 1024 * 1024
        ),
        name="decode",
    )(lengths, query_rows, residual, norm_gain.reshape(GROUP, HD), kv_cache.reshape(2, 3, -1, HD), w_gate_up, w_down)


def solution(mesh):
    return jax.shard_map(
        on_device,
        mesh=mesh,
        in_specs=(
            P(("attn", "fcol"), "frow"),
            P(None, ("attn", "fcol"), None, "frow"),
            P(("attn", "fcol")),
            P(("attn", "fcol"), "frow"),
            P("frow"),
            P(None, ("attn", "fcol"), "frow"),
            P(("attn", "fcol"), "frow"),
        ),
        out_specs=P(("attn", "fcol"), "frow"),
        check_vma=False,
    )
```

time: 766 us -> 72.6 us (0.09)
  the two profiles are of different devices: /device:TPU:1 before, /device:TPU:8 now
where the time goes in v1:
time: 72.6 us; the launch traced here: 72.3 us
  Pallas kernels  64.6 us (89%)
  local copies, waits for them, and re-layouts  7.61 us (10%)
    pallas_call x1, Pallas kernels, on_device(): pl.pallas_call(body, out_shape=jax.ShapeDtypeStruct(query_rows.shape, bf1...  64.6 us
    unnamed x15, local copies, waits for them, and re-layouts  7.61 us

profile of v1, /device:TPU:8, one launch (start us, length us, event | category | flops | bytes accessed | tf_op | source)
XLA Modules:
  0.0 72.3 jit_solution(178708127545216975)
XLA Ops:
  0.0 0.0 copy-start
  0.0 1.6 %copy-done = bf16[2,256,2048]{2,1,0:T(8,128)(2,1)S(1)} copy-done((bf16[2,256,2048]{2,1,0:T(8,128)(2,1)S(1)}, bf16[2,256,2048]{2,1,0:T(8,128)(2,1)}, u32[]{:S(2)}) %copy-start) | copy-done | bytes 2097176
  1.6 0.0 copy-start.1
  1.6 1.4 %copy-done.1 = bf16[2,3,1024,128]{3,2,1,0:T(8,128)(2,1)S(1)} copy-done((bf16[2,3,1024,128]{3,2,1,0:T(8,128)(2,1)S(1)}, bf16[2,3,1024,128]{3,2,1,0:T(8,128)(2,1)}, u32[]{:S(2)}) %copy-start.1) | copy-done | bytes 1572888
  3.0 0.0 copy-start.2
  3.0 1.2 %copy-done.2 = bf16[256,2048]{1,0:T(8,128)(2,1)S(1)} copy-done((bf16[256,2048]{1,0:T(8,128)(2,1)S(1)}, bf16[256,2048]{1,0:T(8,128)(2,1)}, u32[]{:S(2)}) %copy-start.2) | copy-done | bytes 1048600
  4.2 0.0 copy-start.3
  4.2 0.7 copy-done.3
  4.9 0.0 copy-start.4
  4.9 0.7 copy-done.4
  5.7 0.0 copy-start.5
  5.7 0.7 copy-done.5
  6.4 0.0 copy-start.6
  6.4 0.7 copy-done.6
  7.0 64.6 %decode.1 = bf16[3,2048]{1,0:T(4,128)(2,1)S(1)} custom-call(s32[3]{0:T(128)S(1)} %copy-done.6, bf16[3,2048]{1,0:T(4,128)(2,1)S(1)} %copy-done.3, bf16[3,2048]{1,0:T(4,128)(2,1)S(1)} %copy-done.4, f32[16,128]{1,0:T(8,128)S(1)} %bitcast.1, bf16[2,3,1024,128]{3,2,1,0:T(8,128)(2,1)S(1)} %copy-done.1, bf16[2,256,2048]{2,1,0:T(8,128)(2,1)S(1)} %copy-done, ...), custom_call_target="tpu_custom_call" | custom-call | tf_op jit(solution)/shard_map/decode/pallas_call | solution.py:280
  71.7 0.6 copy.9
Async XLA Ops:
  0.0 1.6 %copy-start = (bf16[2,256,2048]{2,1,0:T(8,128)(2,1)S(1)}, bf16[2,256,2048]{2,1,0:T(8,128)(2,1)}, u32[]{:S(2)}) copy-start(bf16[2,256,2048]{2,1,0:T(8,128)(2,1)} %wgu_hbm.1) | copy-start | bytes 6291460
  1.6 1.4 %copy-start.1 = (bf16[2,3,1024,128]{3,2,1,0:T(8,128)(2,1)S(1)}, bf16[2,3,1024,128]{3,2,1,0:T(8,128)(2,1)}, u32[]{:S(2)}) copy-start(bf16[2,3,1024,128]{3,2,1,0:T(8,128)(2,1)} %kv_hbm.1) | copy-start | bytes 4718596
  3.0 1.2 %copy-start.2 = (bf16[256,2048]{1,0:T(8,128)(2,1)S(1)}, bf16[256,2048]{1,0:T(8,128)(2,1)}, u32[]{:S(2)}) copy-start(bf16[256,2048]{1,0:T(8,128)(2,1)} %wd_hbm.1) | copy-start | bytes 3145732
  4.2 0.7 copy-start.3
  4.9 0.7 copy-start.4
  5.7 0.7 copy-start.5
  6.4 0.7 copy-start.6

commit v2 on v1

v2 whole, which is shorter than its diff:
```python
import functools
import math

import jax
import jax.numpy as jnp
from jax import lax
from jax.experimental import pallas as pl
from jax.experimental.pallas import tpu as pltpu
from jax.sharding import PartitionSpec as P

HD = 128
GROUP = 16
MESH = pl.DeviceIdType.MESH
SENDS, LANDS = 16, 37
NT = (((1,), (1,)), ((), ()))

Z_OFFSETS = (0, 1, -1, 2, -2, 3, -3, 4, -4, 5, -5, 6, -6, 7, -7, 8)
Z_SLOT = {o % 16: i for i, o in enumerate(Z_OFFSETS)}
R_OFFSETS = (0, 1, -1, 2)
R_SLOT = {o % 4: i for i, o in enumerate(R_OFFSETS)}
NEAR_RUNS = ((0, 0, 1), (0, 1, 3), (0, 3, 5), (0, 5, 8))
FAR_RUNS = ((1, 0, 1), (1, 1, 3), (1, 3, 5), (1, 5, 8))


def body(len_hbm, q_hbm, res_hbm, gain_hbm, kv_hbm, wgu_hbm, wd_hbm, out_ref,
         len_ref, q_ref, res_ref, gain_ref, kv, wgu, wd, lay, inverse, xb, xt, gu, yr, hb, po, dr, xr, s1, zi, zacc, zf, room,
         local_sem, send_sem, recv_sem):
    attn = lax.axis_index("attn")
    y = lax.axis_index("frow")
    x = lax.axis_index("fcol")
    z, core = attn // 2, attn % 2

    def at_z(offset):
        return {"attn": ((z + offset + 16) % 16) * 2 + core}

    def at_x(offset):
        return {"fcol": (x + offset + 4) % 4}

    def at_y(offset):
        return {"frow": (y + offset + 4) % 4}

    other_core = {"attn": z * 2 + 1 - core}

    barrier = pltpu.get_barrier_semaphore()
    peers = [at_z(o) for o in (4, -4, 3, -3, 2, -2, 1, -1)]
    peers += [at_x(o) for o in R_OFFSETS[1:]] + [at_y(o) for o in R_OFFSETS[1:]] + [other_core]
    for peer in peers:
        pl.semaphore_signal(barrier, inc=1, device_id=peer, device_id_type=MESH)

    operands = (
        (q_hbm, q_ref), (len_hbm, len_ref), (res_hbm, res_ref), (gain_hbm, gain_ref),
        (kv_hbm.at[0], kv.at[0]), (kv_hbm.at[1], kv.at[1]), (wgu_hbm, wgu), (wd_hbm, wd),
    )
    loads = [pltpu.make_async_copy(src, dst, local_sem.at[i]) for i, (src, dst) in enumerate(operands)]
    for load in loads:
        load.start()

    taken = [0, 0]
    sent = []

    def take(kind):
        taken[kind] += 1
        return (send_sem, recv_sem)[kind].at[taken[kind] - 1]

    def outgoing(rows):
        sent.append((take(0), rows))
        return sent[-1][0]

    def remote(src, dst, peer, leaves, lands):
        return pltpu.make_async_remote_copy(
            src_ref=src, dst_ref=dst, send_sem=leaves, recv_sem=lands, device_id=peer, device_id_type=MESH
        )

    def send(src, dst, peer, leaves, lands):
        remote(src, dst, peer, leaves, lands).start()

    def landed(ref, sem):
        pltpu.make_async_copy(ref, ref, sem).wait()

    def spread(rows):
        for r in range(3):
            for h in range(GROUP):
                lay[pl.ds(r * GROUP + h, 1), :] = rows[r:r + 1, h * HD:(h + 1) * HD]
        return lay[...]

    for load in loads[:4]:
        load.wait()
    queries = spread(q_ref[...].astype(jnp.float32)).astype(jnp.bfloat16)
    residual = spread(res_ref[...].astype(jnp.float32))
    gain = gain_ref[...]
    square = 1.0 / (gain * gain)
    for h in range(GROUP):
        inverse[:, h * HD:(h + 1) * HD] = square[h:h + 1]
    loads[4].wait()
    loads[5].wait()
    positions = lax.broadcasted_iota(jnp.int32, (GROUP, kv.shape[2]), 1)
    for r in range(3):
        scores = lax.dot_general(
            queries[r * GROUP:(r + 1) * GROUP], kv[0, r], NT, preferred_element_type=jnp.float32
        ) * (1.0 / math.sqrt(HD))
        live = positions < len_ref[r]
        scores = jnp.where(live, scores, -1e30)
        top = jnp.max(scores, axis=1, keepdims=True)
        expo = jnp.where(live, jnp.exp(scores - top), 0.0)
        total = jnp.sum(expo, axis=1, keepdims=True)
        summed = jnp.dot(expo.astype(jnp.bfloat16), kv[1, r], preferred_element_type=jnp.float32)
        mixed = residual[r * GROUP:(r + 1) * GROUP] + summed / total
        xb[0, 0, 0, 0, r * GROUP:(r + 1) * GROUP, :] = (mixed * gain).astype(jnp.bfloat16)

    pl.semaphore_wait(barrier, len(peers))

    def slot(offset):
        index = Z_SLOT[offset % 16]
        return xb.at[0, index // 8, 0, index % 8]

    z_sem = {}
    for group in ((1, -1), (2, -2), (3, -3), (4,), (-4,), (5, -5), (6, -6), (7, -7, 8)):
        lands = take(1)
        for o in group:
            z_sem[o % 16] = lands
    leaves = outgoing(15 * 48)
    for o in (4, -4, 3, -3, 2, -2, 1, -1):
        send(slot(0), slot(-o), at_z(o), leaves, z_sem[-o % 16])

    x_sem = {run: take(1) for run in NEAR_RUNS + FAR_RUNS}
    core_sem = {run: take(1) for run in NEAR_RUNS + FAR_RUNS}
    x_leaves = [outgoing(8 * 48 * 3), outgoing(8 * 48 * 3)]
    core_leaves = [outgoing(8 * 48 * 4), outgoing(8 * 48 * 4)]

    def along_z(run, count=None):
        chunk, first, end = run
        return xb.at[0, chunk, 0, pl.ds(first, (end - first) if count is None else count)]

    def hand_on_x(run):
        chunk, first, end = run
        if run == NEAR_RUNS[3]:
            landed(along_z(run, 2), z_sem[3])
        elif run not in (NEAR_RUNS[0], FAR_RUNS[0]):
            landed(along_z(run), z_sem[Z_OFFSETS[chunk * 8 + first] % 16])
        here = pl.ds(first, end - first)
        for o in (2, 1, -1):
            send(xb.at[0, chunk, 0, here], xb.at[0, chunk, R_SLOT[-o % 4], here], at_x(o), x_leaves[chunk], x_sem[run])

    def hand_on_core(run):
        chunk, first, end = run
        here = pl.ds(first, end - first)
        landed(xb.at[0, chunk, 1:4, here], x_sem[run])
        send(xb.at[0, chunk, :, here], xb.at[1, chunk, :, here], other_core, core_leaves[chunk], core_sem[run])

    def from_core(run):
        chunk, first, end = run
        landed(xb.at[1, chunk, :, pl.ds(first, end - first)], core_sem[run])

    hand_on_x(NEAR_RUNS[0])
    hand_on_x(NEAR_RUNS[1])
    hand_on_x(NEAR_RUNS[2])
    landed(slot(-4), z_sem[-4 % 16])
    for j in (4, 3, 2, 1):
        send(slot(-4), slot(-(4 + j)), at_z(j), leaves, z_sem[-(4 + j) % 16])
    landed(slot(4), z_sem[4])
    for j in (3, 2, 1):
        send(slot(4), slot(4 + j), at_z(-j), leaves, z_sem[4 + j])
    hand_on_x(NEAR_RUNS[3])
    hand_on_x(FAR_RUNS[0])
    hand_on_core(NEAR_RUNS[0])
    hand_on_core(NEAR_RUNS[1])
    hand_on_x(FAR_RUNS[1])
    hand_on_core(NEAR_RUNS[2])
    hand_on_x(FAR_RUNS[2])
    hand_on_core(NEAR_RUNS[3])
    hand_on_x(FAR_RUNS[3])

    def widen(chunk, p):
        rows = xb[p, chunk].reshape(96, GROUP, HD).reshape(96, GROUP * HD)
        xt[chunk, pl.ds(p * 96, 96), :] = rows
        wide = rows.astype(jnp.float32)
        return jnp.sum(wide * wide * inverse[...], axis=1, keepdims=True)

    lanes = lax.broadcasted_iota(jnp.int32, (96, HD), 1)
    y_sem = [(outgoing(720), take(1)) for _ in range(2)]
    h_sem = [(outgoing(288), take(1)) for _ in range(2)]

    def project(chunk, p, squares):
        high = squares.astype(jnp.bfloat16).astype(jnp.float32)
        both = jnp.where(lanes < 64, high, squares - high).astype(jnp.bfloat16)
        gu[chunk, 2 * p:2 * p + 2, :, 512:640] = both.reshape(2, 48, HD)
        rows = xt[chunk, p * 96:(p + 1) * 96]
        for k in range(2):
            part = lax.dot_general(rows, wgu[k], NT, preferred_element_type=jnp.float32)
            gu[chunk, 2 * p:2 * p + 2, :, k * 256:(k + 1) * 256] = part.astype(jnp.bfloat16).reshape(2, 48, 256)
        for o in (2, 1, -1):
            target = (y + o + 4) % 4
            copy = remote(gu.at[chunk, target], yr.at[chunk, R_SLOT[-o % 4] - 1], at_y(o), *y_sem[chunk])
            pl.when(target // 2 == p)(copy.start)

    def activate(chunk):
        landed(yr.at[chunk], y_sem[chunk][1])
        v = gu[chunk, y].astype(jnp.float32)
        for i in range(3):
            v += yr[chunk, i].astype(jnp.float32)
        meansq = (v[:, 512:513] + v[:, 576:577]) * (1.0 / 8192)
        scale = lax.rsqrt(meansq + 1e-05)
        gate = v[:, :256] * scale
        up = v[:, 256:512] * scale
        hb[chunk, y] = (gate / (1.0 + jnp.exp(-gate)) * up).astype(jnp.bfloat16)
        for o in (2, 1, -1):
            send(hb.at[chunk, y], hb.at[chunk, y], at_y(o), *h_sem[chunk])

    halves = ((slice(None),), (1, 0))
    c_sem = [[(outgoing(1536 // len(h)), take(1)) for _ in h] for h in halves]
    r_sem = [[(outgoing(1152 // len(h)), take(1)) for _ in h] for h in halves]

    def down(chunk):
        landed(hb.at[chunk, 0:3], h_sem[chunk][1])
        for p in (1, 0):
            rows = hb[chunk, 2 * p:2 * p + 2].reshape(96, 256)
            wide = jnp.dot(rows, wd[...], preferred_element_type=jnp.float32).astype(jnp.bfloat16)
            po[p, chunk] = wide.reshape(96, GROUP, HD).reshape(4, 2, 192, HD)
            if p == 1:
                for half, sems in zip(halves[chunk], c_sem[chunk]):
                    send(po.at[1, chunk, :, half], dr.at[chunk, :, half], other_core, *sems)

    def reduce_core(chunk):
        for half, sems, onward in zip(halves[chunk], c_sem[chunk], r_sem[chunk]):
            landed(dr.at[chunk, :, half], sems[1])
            v = po[0, chunk, :, half].astype(jnp.float32) + dr[chunk, :, half].astype(jnp.float32)
            po[0, chunk, :, half] = v.astype(jnp.bfloat16)
            for o in (2, 1, -1):
                send(po.at[0, chunk, R_SLOT[o % 4], half], xr.at[chunk, R_SLOT[-o % 4] - 1, half], at_x(o), *onward)

    def reduce_x(chunk, i):
        half = halves[chunk][i]
        landed(xr.at[chunk, :, half], r_sem[chunk][i][1])
        v = po[0, chunk, 0, half].astype(jnp.float32)
        for k in range(3):
            v += xr[chunk, k, half].astype(jnp.float32)
        s1[chunk, half] = v.astype(jnp.bfloat16).reshape(s1.at[chunk, half].shape)

    def sums(offset):
        index = Z_SLOT[offset % 16]
        return s1.at[index // 8, index // 4 % 2, index % 4]

    last_sem = (outgoing(15 * 48), take(1))
    far_sem = [(last_sem[0], take(1)) for _ in range(2)]

    loads[6].wait()
    squares = widen(0, 0)
    project(0, 0, squares)
    for run in NEAR_RUNS:
        from_core(run)
    squares = widen(0, 1)
    project(0, 1, squares)
    for run in FAR_RUNS:
        hand_on_core(run)
    activate(0)
    squares = widen(1, 0)
    project(1, 0, squares)
    for run in FAR_RUNS:
        from_core(run)
    squares = widen(1, 1)
    project(1, 1, squares)
    loads[7].wait()
    down(0)
    activate(1)
    reduce_core(0)
    down(1)
    reduce_core(1)
    reduce_x(0, 0)
    for i, o in enumerate((3, -3, 2, -2, 1, -1)):
        send(sums(o), zf.at[i], at_z(o), *last_sem)
    reduce_x(1, 0)
    for o in (8, 7, -7, -6):
        j = abs(o) - 4
        send(sums(o), zi.at[j - 1 if o > 0 else 3 + j], at_z(j if o > 0 else -j), *far_sem[0 if o > 0 else 1])
    reduce_x(1, 1)
    for o in (6, 5, -5):
        j = abs(o) - 4
        send(sums(o), zi.at[j - 1 if o > 0 else 3 + j], at_z(j if o > 0 else -j), *far_sem[0 if o > 0 else 1])
    for i, (offset, first, count) in enumerate(((4, 0, 4), (-4, 4, 3))):
        landed(zi.at[pl.ds(first, count)], far_sem[i][1])
        v = sums(offset)[...].astype(jnp.float32)
        for j in range(count):
            v += zi[first + j].astype(jnp.float32)
        zacc[i] = v.astype(jnp.bfloat16)
        send(zacc.at[i], zf.at[6 + i], at_z(offset), *last_sem)
    v = sums(0)[...].astype(jnp.float32)
    landed(zf, last_sem[1])
    for i in range(8):
        v += zf[i].astype(jnp.float32)
    lay[...] = v
    for r in range(3):
        for h in range(GROUP):
            out_ref[r:r + 1, h * HD:(h + 1) * HD] = lay[pl.ds(r * GROUP + h, 1), :].astype(jnp.bfloat16)
    for leaves, rows in sent:
        landed(room.at[pl.ds(0, rows)], leaves)
    assert taken == [SENDS, LANDS], taken


def on_device(query_rows, kv_cache, lengths, residual, norm_gain, w_gate_up, w_down):
    bf16 = jnp.bfloat16
    vmem = pl.BlockSpec(memory_space=pltpu.VMEM)
    hbm = pl.BlockSpec(memory_space=pl.ANY)
    return pl.pallas_call(
        body,
        out_shape=jax.ShapeDtypeStruct(query_rows.shape, bf16),
        in_specs=[hbm] * 7,
        out_specs=vmem,
        scratch_shapes=[
            pltpu.SMEM(lengths.shape, jnp.int32),
            pltpu.VMEM(query_rows.shape, bf16),
            pltpu.VMEM(residual.shape, bf16),
            pltpu.VMEM((GROUP, HD), jnp.float32),
            pltpu.VMEM(kv_cache.shape, bf16),
            pltpu.VMEM(w_gate_up.shape, bf16),
            pltpu.VMEM(w_down.shape, bf16),
            pltpu.VMEM((48, HD), jnp.float32),
            pltpu.VMEM((1, GROUP * HD), jnp.float32),
            pltpu.VMEM((2, 2, 4, 8, 48, HD), bf16),
            pltpu.VMEM((2, 192, 2048), bf16),
            pltpu.VMEM((2, 4, 48, 640), bf16),
            pltpu.VMEM((2, 3, 48, 640), bf16),
            pltpu.VMEM((2, 4, 48, 256), bf16),
            pltpu.VMEM((2, 2, 4, 2, 192, HD), bf16),
            pltpu.VMEM((2, 4, 2, 192, HD), bf16),
            pltpu.VMEM((2, 3, 2, 192, HD), bf16),
            pltpu.VMEM((2, 2, 4, 48, HD), bf16),
            pltpu.VMEM((7, 48, HD), bf16),
            pltpu.VMEM((2, 48, HD), bf16),
            pltpu.VMEM((8, 48, HD), bf16),
            pltpu.VMEM((1536, HD), bf16),
            pltpu.SemaphoreType.DMA((8,)),
            pltpu.SemaphoreType.DMA((SENDS,)),
            pltpu.SemaphoreType.DMA((LANDS,)),
        ],
        compiler_params=pltpu.CompilerParams(
            collective_id=0, has_side_effects=True, vmem_limit_bytes=60 * 1024 * 1024
        ),
        name="decode",
    )(lengths, query_rows, residual, norm_gain.reshape(GROUP, HD), kv_cache.reshape(2, 3, -1, HD), w_gate_up, w_down)


def solution(mesh):
    return jax.shard_map(
        on_device,
        mesh=mesh,
        in_specs=(
            P(("attn", "fcol"), "frow"),
            P(None, ("attn", "fcol"), None, "frow"),
            P(("attn", "fcol")),
            P(("attn", "fcol"), "frow"),
            P("frow"),
            P(None, ("attn", "fcol"), "frow"),
            P(("attn", "fcol"), "frow"),
        ),
        out_specs=P(("attn", "fcol"), "frow"),
        check_vma=False,
    )
```

time: 72.6 us -> 59.8 us (0.82)
  the two profiles are of different devices: /device:TPU:8 before, /device:TPU:1 now
where the time goes in v2:
time: 59.8 us; the launch traced here: 59.5 us
  Pallas kernels  58.1 us (97%)
  local copies, waits for them, and re-layouts  1.33 us (2%)
    pallas_call x1, Pallas kernels, on_device(): pl.pallas_call(body, out_shape=jax.ShapeDtypeStruct(query_rows.shape, bf1...  58.1 us
    unnamed x1, local copies, waits for them, and re-layouts  1.33 us

profile of v2, /device:TPU:1, one launch (start us, length us, event | category | flops | bytes accessed | tf_op | source)
XLA Modules:
  0.0 59.5 jit_solution(28582335552001146)
XLA Ops:
  0.0 58.1 %decode.1 = bf16[3,2048]{1,0:T(4,128)(2,1)} custom-call(s32[3]{0:T(128)} %len_hbm.1, bf16[3,2048]{1,0:T(4,128)(2,1)} %q_hbm.1, bf16[3,2048]{1,0:T(4,128)(2,1)} %res_hbm.1, f32[16,128]{1,0:T(8,128)} %bitcast.1, bf16[2,3,1024,128]{3,2,1,0:T(8,128)(2,1)} %kv_hbm.1, bf16[2,256,2048]{2,1,0:T(8,128)(2,1)} %wgu_hbm.1, bf16[256,2048]{1,0:T(8,128)(2,1)} %wd_hbm.1), custom_call_target="tpu_custom_call" | custom-call | tf_op jit(solution)/shard_map/decode/pallas_call | solution.py:303
  58.2 1.3 %copy.9 = bf16[3,2048]{1,0:T(4,128)(2,1)} copy(bf16[3,2048]{1,0:T(4,128)(2,1)} %decode.1) | data formatting | bytes 24576

commit v3 on v2

--- a/solution.py
+++ b/solution.py
@@ -11,7 +11,7 @@
 HD = 128
 GROUP = 16
 MESH = pl.DeviceIdType.MESH
-SENDS, LANDS = 16, 37
+SENDS, LANDS = 16, 40
 NT = (((1,), (1,)), ((), ()))
 
 Z_OFFSETS = (0, 1, -1, 2, -2, 3, -3, 4, -4, 5, -5, 6, -6, 7, -7, 8)
@@ -19,11 +19,11 @@
 R_OFFSETS = (0, 1, -1, 2)
 R_SLOT = {o % 4: i for i, o in enumerate(R_OFFSETS)}
 NEAR_RUNS = ((0, 0, 1), (0, 1, 3), (0, 3, 5), (0, 5, 8))
-FAR_RUNS = ((1, 0, 1), (1, 1, 3), (1, 3, 5), (1, 5, 8))
+FAR_RUNS = ((1, 0, 1), (1, 1, 3), (1, 3, 5), (1, 5, 7), (1, 7, 8))
 
 
 def body(len_hbm, q_hbm, res_hbm, gain_hbm, kv_hbm, wgu_hbm, wd_hbm, out_ref,
-         len_ref, q_ref, res_ref, gain_ref, kv, wgu, wd, lay, inverse, xb, xt, gu, yr, hb, po, dr, xr, s1, zi, zacc, zf, room,
+         len_ref, q_ref, res_ref, gain_ref, kv, wgu, wt, wd, lay, inverse, xb, xt, gu, yr, hb, po, dr, xr, s1, zi, zacc, zf, room,
          local_sem, send_sem, recv_sem):
     attn = lax.axis_index("attn")
     y = lax.axis_index("frow")
@@ -114,7 +114,7 @@
         return xb.at[0, index // 8, 0, index % 8]
 
     z_sem = {}
-    for group in ((1, -1), (2, -2), (3, -3), (4,), (-4,), (5, -5), (6, -6), (7, -7, 8)):
+    for group in ((1, -1), (2, -2), (3, -3), (4,), (-4,), (5, -5), (6, -6), (7, -7), (8,)):
         lands = take(1)
         for o in group:
             z_sem[o % 16] = lands
@@ -152,6 +152,8 @@
         landed(xb.at[1, chunk, :, pl.ds(first, end - first)], core_sem[run])
 
     hand_on_x(NEAR_RUNS[0])
+    loads[6].wait()
+    wt[0] = wgu[0].T
     hand_on_x(NEAR_RUNS[1])
     hand_on_x(NEAR_RUNS[2])
     landed(slot(-4), z_sem[-4 % 16])
@@ -162,6 +164,7 @@
         send(slot(4), slot(4 + j), at_z(-j), leaves, z_sem[4 + j])
     hand_on_x(NEAR_RUNS[3])
     hand_on_x(FAR_RUNS[0])
+    wt[1] = wgu[1].T
     hand_on_core(NEAR_RUNS[0])
     hand_on_core(NEAR_RUNS[1])
     hand_on_x(FAR_RUNS[1])
@@ -169,6 +172,7 @@
     hand_on_x(FAR_RUNS[2])
     hand_on_core(NEAR_RUNS[3])
     hand_on_x(FAR_RUNS[3])
+    hand_on_x(FAR_RUNS[4])
 
     def widen(chunk, p):
         rows = xb[p, chunk].reshape(96, GROUP, HD).reshape(96, GROUP * HD)
@@ -186,7 +190,7 @@
         gu[chunk, 2 * p:2 * p + 2, :, 512:640] = both.reshape(2, 48, HD)
         rows = xt[chunk, p * 96:(p + 1) * 96]
         for k in range(2):
-            part = lax.dot_general(rows, wgu[k], NT, preferred_element_type=jnp.float32)
+            part = jnp.dot(rows, wt[k], preferred_element_type=jnp.float32)
             gu[chunk, 2 * p:2 * p + 2, :, k * 256:(k + 1) * 256] = part.astype(jnp.bfloat16).reshape(2, 48, 256)
         for o in (2, 1, -1):
             target = (y + o + 4) % 4
@@ -243,7 +247,6 @@
     last_sem = (outgoing(15 * 48), take(1))
     far_sem = [(last_sem[0], take(1)) for _ in range(2)]
 
-    loads[6].wait()
     squares = widen(0, 0)
     project(0, 0, squares)
     for run in NEAR_RUNS:
@@ -252,9 +255,9 @@
     project(0, 1, squares)
     for run in FAR_RUNS:
         hand_on_core(run)
-    activate(0)
     squares = widen(1, 0)
     project(1, 0, squares)
+    activate(0)
     for run in FAR_RUNS:
         from_core(run)
     squares = widen(1, 1)
@@ -302,7 +305,7 @@
     hbm = pl.BlockSpec(memory_space=pl.ANY)
     return pl.pallas_call(
         body,
-        out_shape=jax.ShapeDtypeStruct(query_rows.shape, bf16),
+        out_shape=pltpu.VMEM(query_rows.shape, bf16),
         in_specs=[hbm] * 7,
         out_specs=vmem,
         scratch_shapes=[
@@ -312,6 +315,7 @@
             pltpu.VMEM((GROUP, HD), jnp.float32),
             pltpu.VMEM(kv_cache.shape, bf16),
             pltpu.VMEM(w_gate_up.shape, bf16),
+            pltpu.VMEM((2, GROUP * HD, 256), bf16),
             pltpu.VMEM(w_down.shape, bf16),
             pltpu.VMEM((48, HD), jnp.float32),
             pltpu.VMEM((1, GROUP * HD), jnp.float32),

time: 59.8 us -> 57.3 us (0.958)
  Pallas kernels: 58.1 us -> 56.5 us
  local copies, waits for them, and re-layouts: 1.33 us -> 0.61 us
    pallas_call x1, Pallas kernels: 58.1 us -> 56.5 us  [on_device(): pl.pallas_call(body, out_shape=pltpu.VMEM(query_rows.shape, bf16), in_spe...]
    unnamed x1, local copies, waits for them, and re-layouts: 1.33 us -> 0.61 us
where the time goes in v3:
time: 57.3 us; the launch traced here: 57.1 us
  Pallas kernels  56.5 us (99%)
  local copies, waits for them, and re-layouts  0.61 us (1%)
    pallas_call x1, Pallas kernels, on_device(): pl.pallas_call(body, out_shape=pltpu.VMEM(query_rows.shape, bf16), in_spe...  56.5 us

profile of v3, /device:TPU:1, one launch (start us, length us, event | category | flops | bytes accessed | tf_op | source)
XLA Modules:
  0.0 57.1 jit_solution(17526521714428182894)
XLA Ops:
  0.0 56.5 %decode.1 = bf16[3,2048]{1,0:T(4,128)(2,1)S(1)} custom-call(s32[3]{0:T(128)} %len_hbm.1, bf16[3,2048]{1,0:T(4,128)(2,1)} %q_hbm.1, bf16[3,2048]{1,0:T(4,128)(2,1)} %res_hbm.1, f32[16,128]{1,0:T(8,128)} %bitcast.1, bf16[2,3,1024,128]{3,2,1,0:T(8,128)(2,1)} %kv_hbm.1, bf16[2,256,2048]{2,1,0:T(8,128)(2,1)} %wgu_hbm.1, bf16[256,2048]{1,0:T(8,128)(2,1)} %wd_hbm.1), custom_call_target="tpu_custom_call" | custom-call | tf_op jit(solution)/shard_map/decode/pallas_call | solution.py:306
  56.5 0.6 %copy.9 = bf16[3,2048]{1,0:T(4,128)(2,1)} copy(bf16[3,2048]{1,0:T(4,128)(2,1)S(1)} %decode.1) | data formatting | bytes 24576

commit v4 on v3

--- a/solution.py
+++ b/solution.py
@@ -11,7 +11,7 @@
 HD = 128
 GROUP = 16
 MESH = pl.DeviceIdType.MESH
-SENDS, LANDS = 16, 40
+SENDS, LANDS = 5, 34
 NT = (((1,), (1,)), ((), ()))
 
 Z_OFFSETS = (0, 1, -1, 2, -2, 3, -3, 4, -4, 5, -5, 6, -6, 7, -7, 8)
@@ -93,19 +93,22 @@
         inverse[:, h * HD:(h + 1) * HD] = square[h:h + 1]
     loads[4].wait()
     loads[5].wait()
+    rows = [slice(r * GROUP, (r + 1) * GROUP) for r in range(3)]
     positions = lax.broadcasted_iota(jnp.int32, (GROUP, kv.shape[2]), 1)
-    for r in range(3):
-        scores = lax.dot_general(
-            queries[r * GROUP:(r + 1) * GROUP], kv[0, r], NT, preferred_element_type=jnp.float32
-        ) * (1.0 / math.sqrt(HD))
-        live = positions < len_ref[r]
-        scores = jnp.where(live, scores, -1e30)
-        top = jnp.max(scores, axis=1, keepdims=True)
-        expo = jnp.where(live, jnp.exp(scores - top), 0.0)
-        total = jnp.sum(expo, axis=1, keepdims=True)
-        summed = jnp.dot(expo.astype(jnp.bfloat16), kv[1, r], preferred_element_type=jnp.float32)
-        mixed = residual[r * GROUP:(r + 1) * GROUP] + summed / total
-        xb[0, 0, 0, 0, r * GROUP:(r + 1) * GROUP, :] = (mixed * gain).astype(jnp.bfloat16)
+    live = jnp.concatenate([positions < len_ref[r] for r in range(3)], axis=0)
+    scores = jnp.concatenate(
+        [lax.dot_general(queries[rows[r]], kv[0, r], NT, preferred_element_type=jnp.float32) for r in range(3)], axis=0
+    ) * (1.0 / math.sqrt(HD))
+    scores = jnp.where(live, scores, -1e30)
+    top = jnp.max(scores, axis=1, keepdims=True)
+    expo = jnp.where(live, jnp.exp(scores - top), 0.0)
+    total = jnp.sum(expo, axis=1, keepdims=True)
+    probs = expo.astype(jnp.bfloat16)
+    summed = jnp.concatenate(
+        [jnp.dot(probs[rows[r]], kv[1, r], preferred_element_type=jnp.float32) for r in range(3)], axis=0
+    )
+    mixed = residual + summed / total
+    xb[0, 0, 0, 0] = (mixed * jnp.concatenate([gain] * 3, axis=0)).astype(jnp.bfloat16)
 
     pl.semaphore_wait(barrier, len(peers))
 
@@ -118,14 +121,14 @@
         lands = take(1)
         for o in group:
             z_sem[o % 16] = lands
-    leaves = outgoing(15 * 48)
+    leaves = outgoing(2 * 15 * 48 + 2 * 720 + 2 * 288)
     for o in (4, -4, 3, -3, 2, -2, 1, -1):
         send(slot(0), slot(-o), at_z(o), leaves, z_sem[-o % 16])
 
     x_sem = {run: take(1) for run in NEAR_RUNS + FAR_RUNS}
-    core_sem = {run: take(1) for run in NEAR_RUNS + FAR_RUNS}
-    x_leaves = [outgoing(8 * 48 * 3), outgoing(8 * 48 * 3)]
-    core_leaves = [outgoing(8 * 48 * 4), outgoing(8 * 48 * 4)]
+    core_sem = [take(1), take(1)]
+    x_leaves = outgoing(2 * 8 * 48 * 3)
+    core_leaves = outgoing(2 * 8 * 48 * 4)
 
     def along_z(run, count=None):
         chunk, first, end = run
@@ -139,17 +142,16 @@
             landed(along_z(run), z_sem[Z_OFFSETS[chunk * 8 + first] % 16])
         here = pl.ds(first, end - first)
         for o in (2, 1, -1):
-            send(xb.at[0, chunk, 0, here], xb.at[0, chunk, R_SLOT[-o % 4], here], at_x(o), x_leaves[chunk], x_sem[run])
+            send(xb.at[0, chunk, 0, here], xb.at[0, chunk, R_SLOT[-o % 4], here], at_x(o), x_leaves, x_sem[run])
 
     def hand_on_core(run):
         chunk, first, end = run
         here = pl.ds(first, end - first)
         landed(xb.at[0, chunk, 1:4, here], x_sem[run])
-        send(xb.at[0, chunk, :, here], xb.at[1, chunk, :, here], other_core, core_leaves[chunk], core_sem[run])
-
-    def from_core(run):
-        chunk, first, end = run
-        landed(xb.at[1, chunk, :, pl.ds(first, end - first)], core_sem[run])
+        send(xb.at[0, chunk, :, here], xb.at[1, chunk, :, here], other_core, core_leaves, core_sem[chunk])
+
+    def from_core(chunk):
+        landed(xb.at[1, chunk], core_sem[chunk])
 
     hand_on_x(NEAR_RUNS[0])
     loads[6].wait()
@@ -157,10 +159,10 @@
     hand_on_x(NEAR_RUNS[1])
     hand_on_x(NEAR_RUNS[2])
     landed(slot(-4), z_sem[-4 % 16])
-    for j in (4, 3, 2, 1):
+    landed(slot(4), z_sem[4])
+    send(xb.at[0, 1 - core, 0, 7 * core], slot(8), at_z(4 - 8 * core), leaves, z_sem[8])
+    for j in (3, 2, 1):
         send(slot(-4), slot(-(4 + j)), at_z(j), leaves, z_sem[-(4 + j) % 16])
-    landed(slot(4), z_sem[4])
-    for j in (3, 2, 1):
         send(slot(4), slot(4 + j), at_z(-j), leaves, z_sem[4 + j])
     hand_on_x(NEAR_RUNS[3])
     hand_on_x(FAR_RUNS[0])
@@ -181,8 +183,13 @@
         return jnp.sum(wide * wide * inverse[...], axis=1, keepdims=True)
 
     lanes = lax.broadcasted_iota(jnp.int32, (96, HD), 1)
-    y_sem = [(outgoing(720), take(1)) for _ in range(2)]
-    h_sem = [(outgoing(288), take(1)) for _ in range(2)]
+    y_sem = [(leaves, take(1)) for _ in range(2)]
+    h_sem = [(leaves, take(1)) for _ in range(2)]
+
+    def block_of(row):
+        return row % 2 * 2 + row // 2
+
+    block = block_of(y)
 
     def project(chunk, p, squares):
         high = squares.astype(jnp.bfloat16).astype(jnp.float32)
@@ -194,25 +201,26 @@
             gu[chunk, 2 * p:2 * p + 2, :, k * 256:(k + 1) * 256] = part.astype(jnp.bfloat16).reshape(2, 48, 256)
         for o in (2, 1, -1):
             target = (y + o + 4) % 4
-            copy = remote(gu.at[chunk, target], yr.at[chunk, R_SLOT[-o % 4] - 1], at_y(o), *y_sem[chunk])
-            pl.when(target // 2 == p)(copy.start)
+            copy = remote(gu.at[chunk, block_of(target)], yr.at[chunk, R_SLOT[-o % 4] - 1], at_y(o), *y_sem[chunk])
+            pl.when(target % 2 == p)(copy.start)
 
     def activate(chunk):
         landed(yr.at[chunk], y_sem[chunk][1])
-        v = gu[chunk, y].astype(jnp.float32)
+        v = gu[chunk, block].astype(jnp.float32)
         for i in range(3):
             v += yr[chunk, i].astype(jnp.float32)
         meansq = (v[:, 512:513] + v[:, 576:577]) * (1.0 / 8192)
         scale = lax.rsqrt(meansq + 1e-05)
         gate = v[:, :256] * scale
         up = v[:, 256:512] * scale
-        hb[chunk, y] = (gate / (1.0 + jnp.exp(-gate)) * up).astype(jnp.bfloat16)
+        hb[chunk, block] = (gate / (1.0 + jnp.exp(-gate)) * up).astype(jnp.bfloat16)
         for o in (2, 1, -1):
-            send(hb.at[chunk, y], hb.at[chunk, y], at_y(o), *h_sem[chunk])
+            send(hb.at[chunk, block], hb.at[chunk, block], at_y(o), *h_sem[chunk])
 
     halves = ((slice(None),), (1, 0))
-    c_sem = [[(outgoing(1536 // len(h)), take(1)) for _ in h] for h in halves]
-    r_sem = [[(outgoing(1152 // len(h)), take(1)) for _ in h] for h in halves]
+    c_leaves, r_leaves = outgoing(2 * 1536), outgoing(2 * 1152)
+    c_sem = [[(c_leaves, take(1)) for _ in h] for h in halves]
+    r_sem = [[(r_leaves, take(1)) for _ in h] for h in halves]
 
     def down(chunk):
         landed(hb.at[chunk, 0:3], h_sem[chunk][1])
@@ -244,13 +252,12 @@
         index = Z_SLOT[offset % 16]
         return s1.at[index // 8, index // 4 % 2, index % 4]
 
-    last_sem = (outgoing(15 * 48), take(1))
-    far_sem = [(last_sem[0], take(1)) for _ in range(2)]
+    last_sem = (leaves, take(1))
+    far_sem = [(last_sem[0], take(1)) for _ in range(3)]
 
     squares = widen(0, 0)
     project(0, 0, squares)
-    for run in NEAR_RUNS:
-        from_core(run)
+    from_core(0)
     squares = widen(0, 1)
     project(0, 1, squares)
     for run in FAR_RUNS:
@@ -258,8 +265,7 @@
     squares = widen(1, 0)
     project(1, 0, squares)
     activate(0)
-    for run in FAR_RUNS:
-        from_core(run)
+    from_core(1)
     squares = widen(1, 1)
     project(1, 1, squares)
     loads[7].wait()
@@ -272,17 +278,20 @@
     for i, o in enumerate((3, -3, 2, -2, 1, -1)):
         send(sums(o), zf.at[i], at_z(o), *last_sem)
     reduce_x(1, 0)
-    for o in (8, 7, -7, -6):
+    send(sums(8), zi.at[3], at_z(4 - 8 * core), *far_sem[2])
+    for o in (7, -7, -6):
         j = abs(o) - 4
         send(sums(o), zi.at[j - 1 if o > 0 else 3 + j], at_z(j if o > 0 else -j), *far_sem[0 if o > 0 else 1])
     reduce_x(1, 1)
     for o in (6, 5, -5):
         j = abs(o) - 4
         send(sums(o), zi.at[j - 1 if o > 0 else 3 + j], at_z(j if o > 0 else -j), *far_sem[0 if o > 0 else 1])
-    for i, (offset, first, count) in enumerate(((4, 0, 4), (-4, 4, 3))):
-        landed(zi.at[pl.ds(first, count)], far_sem[i][1])
-        v = sums(offset)[...].astype(jnp.float32)
-        for j in range(count):
+    landed(zi.at[3], far_sem[2][1])
+    farthest = zi[3].astype(jnp.float32)
+    for i, (offset, first) in enumerate(((4, 0), (-4, 4))):
+        landed(zi.at[pl.ds(first, 3)], far_sem[i][1])
+        v = sums(offset)[...].astype(jnp.float32) + jnp.where(core == i, farthest, 0.0)
+        for j in range(3):
             v += zi[first + j].astype(jnp.float32)
         zacc[i] = v.astype(jnp.bfloat16)
         send(zacc.at[i], zf.at[6 + i], at_z(offset), *last_sem)
@@ -331,7 +340,7 @@
             pltpu.VMEM((7, 48, HD), bf16),
             pltpu.VMEM((2, 48, HD), bf16),
             pltpu.VMEM((8, 48, HD), bf16),
-            pltpu.VMEM((1536, HD), bf16),
+            pltpu.VMEM((3456, HD), bf16),
             pltpu.SemaphoreType.DMA((8,)),
             pltpu.SemaphoreType.DMA((SENDS,)),
             pltpu.SemaphoreType.DMA((LANDS,)),

time: 57.3 us -> 57.1 us (level)
  no operation moved by 1% of the time
where the time goes in v4:
time: 57.1 us; the launch traced here: 56.9 us
  Pallas kernels  56.3 us (99%)
  local copies, waits for them, and re-layouts  0.61 us (1%)
    pallas_call x1, Pallas kernels, on_device(): pl.pallas_call(body, out_shape=pltpu.VMEM(query_rows.shape, bf16), in_spe...  56.3 us

profile of v4, /device:TPU:1, one launch (start us, length us, event | category | flops | bytes accessed | tf_op | source)
XLA Modules:
  0.0 56.9 jit_solution(11900009275078718634)
XLA Ops:
  0.0 56.3 %decode.1 = bf16[3,2048]{1,0:T(4,128)(2,1)S(1)} custom-call(s32[3]{0:T(128)} %len_hbm.1, bf16[3,2048]{1,0:T(4,128)(2,1)} %q_hbm.1, bf16[3,2048]{1,0:T(4,128)(2,1)} %res_hbm.1, f32[16,128]{1,0:T(8,128)} %bitcast.1, bf16[2,3,1024,128]{3,2,1,0:T(8,128)(2,1)} %kv_hbm.1, bf16[2,256,2048]{2,1,0:T(8,128)(2,1)} %wgu_hbm.1, bf16[256,2048]{1,0:T(8,128)(2,1)} %wd_hbm.1), custom_call_target="tpu_custom_call" | custom-call | tf_op jit(solution)/shard_map/decode/pallas_call | solution.py:315
  56.3 0.6 %copy.9 = bf16[3,2048]{1,0:T(4,128)(2,1)} copy(bf16[3,2048]{1,0:T(4,128)(2,1)S(1)} %decode.1) | data formatting | bytes 24576

commit v5 on v4

--- a/solution.py
+++ b/solution.py
@@ -11,7 +11,7 @@
 HD = 128
 GROUP = 16
 MESH = pl.DeviceIdType.MESH
-SENDS, LANDS = 5, 34
+SENDS, LANDS = 5, 36
 NT = (((1,), (1,)), ((), ()))
 
 Z_OFFSETS = (0, 1, -1, 2, -2, 3, -3, 4, -4, 5, -5, 6, -6, 7, -7, 8)
@@ -23,7 +23,7 @@
 
 
 def body(len_hbm, q_hbm, res_hbm, gain_hbm, kv_hbm, wgu_hbm, wd_hbm, out_ref,
-         len_ref, q_ref, res_ref, gain_ref, kv, wgu, wt, wd, lay, inverse, xb, xt, gu, yr, hb, po, dr, xr, s1, zi, zacc, zf, room,
+         len_ref, q_ref, res_ref, gain_ref, kv, wgu, wt, wd, lay, inverse, xb, xt, gu, yr, sq, sr, hb, po, dr, xr, s1, zi, zacc, zf, room,
          local_sem, send_sem, recv_sem):
     attn = lax.axis_index("attn")
     y = lax.axis_index("frow")
@@ -121,7 +121,7 @@
         lands = take(1)
         for o in group:
             z_sem[o % 16] = lands
-    leaves = outgoing(2 * 15 * 48 + 2 * 720 + 2 * 288)
+    leaves = outgoing(2 * 15 * 48 + 2 * 576 + 2 * 48 + 2 * 288)
     for o in (4, -4, 3, -3, 2, -2, 1, -1):
         send(slot(0), slot(-o), at_z(o), leaves, z_sem[-o % 16])
 
@@ -183,7 +183,10 @@
         return jnp.sum(wide * wide * inverse[...], axis=1, keepdims=True)
 
     lanes = lax.broadcasted_iota(jnp.int32, (96, HD), 1)
+    diagonal = lax.broadcasted_iota(jnp.int32, (48, HD), 0) == lax.broadcasted_iota(jnp.int32, (48, HD), 1)
+    upper = lax.broadcasted_iota(jnp.int32, (16, HD), 0) < 8
     y_sem = [(leaves, take(1)) for _ in range(2)]
+    sq_sem = [take(1) for _ in range(2)]
     h_sem = [(leaves, take(1)) for _ in range(2)]
 
     def block_of(row):
@@ -194,7 +197,11 @@
     def project(chunk, p, squares):
         high = squares.astype(jnp.bfloat16).astype(jnp.float32)
         both = jnp.where(lanes < 64, high, squares - high).astype(jnp.bfloat16)
-        gu[chunk, 2 * p:2 * p + 2, :, 512:640] = both.reshape(2, 48, HD)
+        for b in range(2):
+            tall = both[b * 48:(b + 1) * 48].astype(jnp.float32)
+            flat = jnp.sum(jnp.where(diagonal, tall[:, 0:1], 0.0), axis=0, keepdims=True)
+            rest = jnp.sum(jnp.where(diagonal, tall[:, 64:65], 0.0), axis=0, keepdims=True)
+            sq[chunk, 2 * p + b] = jnp.where(upper, flat, rest).astype(jnp.bfloat16)
         rows = xt[chunk, p * 96:(p + 1) * 96]
         for k in range(2):
             part = jnp.dot(rows, wt[k], preferred_element_type=jnp.float32)
@@ -202,6 +209,8 @@
         for o in (2, 1, -1):
             target = (y + o + 4) % 4
             copy = remote(gu.at[chunk, block_of(target)], yr.at[chunk, R_SLOT[-o % 4] - 1], at_y(o), *y_sem[chunk])
+            small = remote(sq.at[chunk, block_of(target)], sr.at[chunk, R_SLOT[-o % 4] - 1], at_y(o), leaves, sq_sem[chunk])
+            pl.when(target % 2 == p)(small.start)
             pl.when(target % 2 == p)(copy.start)
 
     def activate(chunk):
@@ -209,7 +218,12 @@
         v = gu[chunk, block].astype(jnp.float32)
         for i in range(3):
             v += yr[chunk, i].astype(jnp.float32)
-        meansq = (v[:, 512:513] + v[:, 576:577]) * (1.0 / 8192)
+        landed(sr.at[chunk], sq_sem[chunk])
+        flat = sq[chunk, block].astype(jnp.float32)
+        for i in range(3):
+            flat += sr[chunk, i].astype(jnp.float32)
+        both = flat[0:1] + flat[8:9]
+        meansq = jnp.sum(jnp.where(diagonal, both, 0.0), axis=1, keepdims=True) * (1.0 / 8192)
         scale = lax.rsqrt(meansq + 1e-05)
         gate = v[:, :256] * scale
         up = v[:, 256:512] * scale
@@ -330,8 +344,10 @@
             pltpu.VMEM((1, GROUP * HD), jnp.float32),
             pltpu.VMEM((2, 2, 4, 8, 48, HD), bf16),
             pltpu.VMEM((2, 192, 2048), bf16),
-            pltpu.VMEM((2, 4, 48, 640), bf16),
-            pltpu.VMEM((2, 3, 48, 640), bf16),
+            pltpu.VMEM((2, 4, 48, 512), bf16),
+            pltpu.VMEM((2, 3, 48, 512), bf16),
+            pltpu.VMEM((2, 4, 16, HD), bf16),
+            pltpu.VMEM((2, 3, 16, HD), bf16),
             pltpu.VMEM((2, 4, 48, 256), bf16),
             pltpu.VMEM((2, 2, 4, 2, 192, HD), bf16),
             pltpu.VMEM((2, 4, 2, 192, HD), bf16),

time: 57.1 us -> 56.6 us (level)
  no operation moved by 1% of the time
where the time goes in v5:
time: 56.6 us; the launch traced here: 56.4 us
  Pallas kernels  55.8 us (99%)
  local copies, waits for them, and re-layouts  0.61 us (1%)
    pallas_call x1, Pallas kernels, on_device(): pl.pallas_call(body, out_shape=pltpu.VMEM(query_rows.shape, bf16), in_spe...  55.8 us

profile of v5, /device:TPU:1, one launch (start us, length us, event | category | flops | bytes accessed | tf_op | source)
XLA Modules:
  0.0 56.4 jit_solution(6818314703073193643)
XLA Ops:
  0.0 55.8 %decode.1 = bf16[3,2048]{1,0:T(4,128)(2,1)S(1)} custom-call(s32[3]{0:T(128)} %len_hbm.1, bf16[3,2048]{1,0:T(4,128)(2,1)} %q_hbm.1, bf16[3,2048]{1,0:T(4,128)(2,1)} %res_hbm.1, f32[16,128]{1,0:T(8,128)} %bitcast.1, bf16[2,3,1024,128]{3,2,1,0:T(8,128)(2,1)} %kv_hbm.1, bf16[2,256,2048]{2,1,0:T(8,128)(2,1)} %wgu_hbm.1, bf16[256,2048]{1,0:T(8,128)(2,1)} %wd_hbm.1), custom_call_target="tpu_custom_call" | custom-call | tf_op jit(solution)/shard_map/decode/pallas_call | solution.py:329
  55.8 0.6 %copy.9 = bf16[3,2048]{1,0:T(4,128)(2,1)} copy(bf16[3,2048]{1,0:T(4,128)(2,1)S(1)} %decode.1) | data formatting | bytes 24576

commit v6 on v5

--- a/solution.py
+++ b/solution.py
@@ -203,15 +203,20 @@
             rest = jnp.sum(jnp.where(diagonal, tall[:, 64:65], 0.0), axis=0, keepdims=True)
             sq[chunk, 2 * p + b] = jnp.where(upper, flat, rest).astype(jnp.bfloat16)
         rows = xt[chunk, p * 96:(p + 1) * 96]
+        targets = [(o, (y + o + 4) % 4) for o in (2, 1, -1)]
+        for o, target in targets:
+            small = remote(sq.at[chunk, block_of(target)], sr.at[chunk, R_SLOT[-o % 4] - 1], at_y(o), leaves, sq_sem[chunk])
+            pl.when(target % 2 == p)(small.start)
         for k in range(2):
+            columns = pl.ds(k * 256, 256)
             part = jnp.dot(rows, wt[k], preferred_element_type=jnp.float32)
             gu[chunk, 2 * p:2 * p + 2, :, k * 256:(k + 1) * 256] = part.astype(jnp.bfloat16).reshape(2, 48, 256)
-        for o in (2, 1, -1):
-            target = (y + o + 4) % 4
-            copy = remote(gu.at[chunk, block_of(target)], yr.at[chunk, R_SLOT[-o % 4] - 1], at_y(o), *y_sem[chunk])
-            small = remote(sq.at[chunk, block_of(target)], sr.at[chunk, R_SLOT[-o % 4] - 1], at_y(o), leaves, sq_sem[chunk])
-            pl.when(target % 2 == p)(small.start)
-            pl.when(target % 2 == p)(copy.start)
+            for o, target in targets:
+                copy = remote(
+                    gu.at[chunk, block_of(target), :, columns], yr.at[chunk, R_SLOT[-o % 4] - 1, :, columns],
+                    at_y(o), *y_sem[chunk],
+                )
+                pl.when(target % 2 == p)(copy.start)
 
     def activate(chunk):
         landed(yr.at[chunk], y_sem[chunk][1])

time: 56.6 us -> 57.1 us (level)
  no operation moved by 1% of the time
where the time goes in v6:
time: 57.1 us; the launch traced here: 56.9 us
  Pallas kernels  56.3 us (99%)
  local copies, waits for them, and re-layouts  0.61 us (1%)
    pallas_call x1, Pallas kernels, on_device(): pl.pallas_call(body, out_shape=pltpu.VMEM(query_rows.shape, bf16), in_spe...  56.3 us

profile of v6, /device:TPU:1, one launch (start us, length us, event | category | flops | bytes accessed | tf_op | source)
XLA Modules:
  0.0 56.9 jit_solution(11775879866260748048)
XLA Ops:
  0.0 56.3 %decode.1 = bf16[3,2048]{1,0:T(4,128)(2,1)S(1)} custom-call(s32[3]{0:T(128)} %len_hbm.1, bf16[3,2048]{1,0:T(4,128)(2,1)} %q_hbm.1, bf16[3,2048]{1,0:T(4,128)(2,1)} %res_hbm.1, f32[16,128]{1,0:T(8,128)} %bitcast.1, bf16[2,3,1024,128]{3,2,1,0:T(8,128)(2,1)} %kv_hbm.1, bf16[2,256,2048]{2,1,0:T(8,128)(2,1)} %wgu_hbm.1, bf16[256,2048]{1,0:T(8,128)(2,1)} %wd_hbm.1), custom_call_target="tpu_custom_call" | custom-call | tf_op jit(solution)/shard_map/decode/pallas_call | solution.py:334
  56.3 0.6 %copy.9 = bf16[3,2048]{1,0:T(4,128)(2,1)} copy(bf16[3,2048]{1,0:T(4,128)(2,1)S(1)} %decode.1) | data formatting | bytes 24576
